TPU v7x, 32 devices: a whole 2x2x4 slice. The times are simulated.
32 devices in a mesh: grp: 2 (over y), wide: 4 (over z), lev: 2 (over x), sub: 2 (over core).
Axes of the slice: x: 2, y: 2, z: 4, core: 2. Of those that a mesh axis runs over, the one named last changes fastest.
Arguments:
- air_state: float32 [8, 32, 512], P('lev', ('grp', 'sub'), 'wide'), parts along dimension 1, may hold values from -6 to 6
- diffusivity: float32 [32, 512], P(('grp', 'sub'), 'wide'), parts along dimension 0, may hold values from 0.25 to 2
- absorber: float32 [7, 8, 32, 512], P(None, 'lev', ('grp', 'sub'), 'wide'), parts along dimension 2, may hold values from 0 to 1
- thickness: float32 [8, 32, 512], P('lev', ('grp', 'sub'), 'wide'), parts along dimension 1, may hold values from 0.5 to 1.5
- cos_zenith: float32 [32, 512], P(('grp', 'sub'), 'wide'), parts along dimension 0, may hold values from 0.1 to 1
- sunlit: int32 [32, 512], P(('grp', 'sub'), 'wide'), parts along dimension 0, may hold values from 0 to 1, as said below
- absorb_coef: float32 [7, 224], replicated, may hold values from 0.0005 to 0.2
- solar_weight: float32 [224], replicated, may hold values from 0.2 to 2
Outputs:
- heating_rate: float32 [8, 32, 512], P('lev', ('grp', 'sub'), 'wide'), parts along dimension 1
- new_state: float32 [8, 32, 512], P('lev', ('grp', 'sub'), 'wide'), parts along dimension 1
There are 2 independent parts, one for each index of `grp`. A program takes and returns all parts, laid end to end along the dimension named above; an argument that names none is the same for every part. Nothing has to cross between parts.
Inputs may be any that keep to these rules, and one draw needn't show every extreme that they name: For the columns of one device's block of 8 x 128 grid points and the block at the same y position half of the x devices away, the two blocks together hold at most 1024 sunlit columns; some block is wholly sunlit and some pair reaches 1024.
All inputs are finite; a program needn't handle non-finite values.
Results may differ from a plain program's by a relative error of at most 0.0003.
Values sent between devices are 32-bit elements; how exact they have to be, the bound alone decides.
No kernel may reach another device: no remote copies, remote signals or barrier semaphores. Data moves between devices by JAX's collectives and lax.ppermute only.
A program may use at most 64 MiB of HBM per device.

v0:
```python
import math

import jax
import jax.numpy as jnp
import numpy as np
from jax import lax
from jax.sharding import PartitionSpec as P

gll_weights = np.array([1.0 / 6.0, 5.0 / 6.0, 5.0 / 6.0, 1.0 / 6.0])
mass_points = np.array([1.0 / 3.0, 5.0 / 6.0, 5.0 / 6.0, 1.0 / 3.0])
time_step = 0.004
high = lax.Precision.HIGHEST


def carried_in(part, axis, combine, identity):
    place = lax.axis_index(axis)
    gathered = lax.all_gather(part, axis)
    state = jnp.zeros_like(part) + jnp.asarray(identity, part.dtype)

    def one(turn, state):
        return combine(state, lax.dynamic_index_in_dim(gathered, turn, 0, False))

    return lax.fori_loop(0, place, one, state)


def padded_2(array, sides, width):
    for axis, dim in sides:
        size, length = (lax.axis_size(axis), array.shape[dim])
        up = [(i, (i + 1) % size) for i in range(size)]
        down = [(j, i) for i, j in up]
        last = lax.slice_in_dim(array, length - width, length, axis=dim)
        initial = lax.slice_in_dim(array, 0, width, axis=dim)
        before = lax.ppermute(last, axis, up)
        after = lax.ppermute(initial, axis, down)
        array = jnp.concatenate([before, array, after], axis=dim)
    return array


def from_behind(block, axis, distance):
    devices = range(lax.axis_size(axis))
    route = [((i - distance) % len(devices), i) for i in devices]
    return lax.ppermute(block, axis, route)


def derivative_table():
    root_five = math.sqrt(5.0)
    outer_big = (5.0 + 5.0 * root_five) / 4.0
    outer_small = (5.0 * root_five - 5.0) / 4.0
    inner_big = (1.0 + root_five) / 4.0
    inner_mid = root_five / 2.0
    inner_small = (root_five - 1.0) / 4.0
    return np.array(
        [
            [-3.0, outer_big, -outer_small, 0.5],
            [-inner_big, 0.0, inner_mid, -inner_small],
            [inner_small, -inner_mid, 0.0, inner_big],
            [-0.5, outer_small, -outer_big, 3.0],
        ]
    )


def radiate(amount, layers, zenith, absorb_coef, solar_weight):
    tau = jnp.einsum("skc,sg->kgc", amount, absorb_coef, precision=high)
    trans = jnp.exp(-tau / zenith)
    inclusive = jnp.cumprod(trans, axis=0)
    local_above = jnp.concatenate(
        [jnp.ones((1,) + trans.shape[1:], jnp.float32), inclusive[:-1]], axis=0
    )
    through = inclusive[-1]
    upper = carried_in(
        through, "lev", lambda earlier, later: earlier * later, jnp.ones_like(through)
    )
    absorbed = zenith * (upper[None] * local_above) * (1.0 - trans)
    return jnp.einsum("kgc,g->kc", absorbed, solar_weight, precision=high) / layers


def edge_masks(rows, width):
    points = 4
    first_x = (jnp.arange(width) % points == 0).astype(jnp.float32)
    last_x = (jnp.arange(width) % points == points - 1).astype(jnp.float32)
    first_y = (jnp.arange(rows) % points == 0).astype(jnp.float32)[:, None]
    last_y = (jnp.arange(rows) % points == points - 1).astype(jnp.float32)[:, None]
    return (first_x, last_x, first_y, last_y)


def assemble(field):
    first_x, last_x, first_y, last_y = edge_masks(field.shape[1], field.shape[2])
    padded = padded_2(field, (("wide", 2),), 1)
    summed = field + first_x * padded[:, :, :-2] + last_x * padded[:, :, 2:]
    padded_y = padded_2(summed, (("sub", 1),), 1)
    return summed + first_y * padded_y[:, :-2] + last_y * padded_y[:, 2:]


def tendency(field, diffusivity, tables):
    block_x, block_y, weight_x, weight_y, mass_grid = tables
    grad_x = jnp.dot(field, block_x.T, precision=high)
    flux_x = diffusivity * weight_x * grad_x
    part_x = -weight_y * jnp.dot(flux_x, block_x, precision=high)
    grad_y = jnp.einsum("qj,ljx->lqx", block_y, field, precision=high)
    flux_y = diffusivity * weight_y * grad_y
    part_y = -weight_x * jnp.einsum("qj,lqx->ljx", block_y, flux_y, precision=high)
    return assemble(part_x + part_y) / mass_grid


def shards(
    air_state, diffusivity, absorber, thickness, cos_zenith, sunlit, absorb_coef, solar_weight
):
    levd, rows, width = air_state.shape
    species = absorber.shape[0]
    table = derivative_table()
    points = table.shape[0]
    columns = rows * width
    keep = columns // 2
    block_x = jnp.asarray(np.kron(np.eye(width // points), table), jnp.float32)
    block_y = jnp.asarray(np.kron(np.eye(rows // points), table), jnp.float32)
    weight_x = jnp.asarray(np.tile(gll_weights, width // points), jnp.float32)
    weight_y = jnp.asarray(np.tile(gll_weights, rows // points), jnp.float32)[:, None]
    mass_grid = jnp.asarray(
        np.outer(np.tile(mass_points, rows // points), np.tile(mass_points, width // points)),
        jnp.float32,
    )
    tables = (block_x, block_y, weight_x, weight_y, mass_grid)
    first_tend = tendency(air_state, diffusivity, tables)
    flat_lit = sunlit.reshape(columns)
    amount_flat = absorber.reshape(species * levd, columns)
    layer_flat = thickness.reshape(levd, columns)
    zenith_flat = cos_zenith.reshape(columns)
    lit_count = jnp.sum(flat_lit)
    own_index = jnp.nonzero(flat_lit, size=columns, fill_value=0)[0].astype(jnp.int32)
    packed = jnp.concatenate(
        [
            jnp.take(amount_flat, own_index, axis=1),
            jnp.take(layer_flat, own_index, axis=1),
            jnp.take(zenith_flat, own_index)[None, :],
        ],
        axis=0,
    )
    half_wide = lax.axis_size("wide") // 2
    arrived = from_behind(packed[:, keep:], "wide", half_wide)
    slot_ids = jnp.arange(keep, dtype=jnp.int32)
    source = jnp.clip(slot_ids - lit_count, 0, keep - 1)
    from_mate = (slot_ids >= lit_count)[None, :]
    merged = jnp.where(from_mate, jnp.take(arrived, source, axis=1), packed[:, :keep])
    heat_slots = radiate(
        merged[: species * levd].reshape(species, levd, keep),
        merged[species * levd : species * levd + levd],
        merged[-1],
        absorb_coef,
        solar_weight,
    )
    outgoing = jnp.take(heat_slots, jnp.clip(slot_ids + lit_count, 0, keep - 1), axis=1)
    returned = from_behind(outgoing, "wide", half_wide)
    heat_list = jnp.concatenate([heat_slots, returned], axis=1)
    rank_ids = jnp.clip(jnp.cumsum(flat_lit) - 1, 0, columns - 1)
    heat_take = jnp.take(heat_list, rank_ids, axis=1)
    heat_cols = jnp.where(flat_lit[None, :] == 1, heat_take, jnp.zeros_like(heat_take))
    heating_rate = heat_cols.reshape(levd, rows, width)
    first = air_state + time_step * (first_tend + heating_rate)
    new_state = 0.5 * (
        air_state + first + time_step * (tendency(first, diffusivity, tables) + heating_rate)
    )
    return (heating_rate, new_state)


def solution(mesh):
    in_specs = (
        P("lev", ("grp", "sub"), "wide"),
        P(("grp", "sub"), "wide"),
        P(None, "lev", ("grp", "sub"), "wide"),
        P("lev", ("grp", "sub"), "wide"),
        P(("grp", "sub"), "wide"),
        P(("grp", "sub"), "wide"),
        P(),
        P(),
    )
    out_specs = (P("lev", ("grp", "sub"), "wide"), P("lev", ("grp", "sub"), "wide"))
    return jax.shard_map(shards, mesh=mesh, in_specs=in_specs, out_specs=out_specs, check_vma=False)
```

profile of v0, /device:TPU:0, one launch (start us, length us, event | category | flops | bytes accessed | tf_op | source)
XLA Modules:
  0.0 95.9 jit_solution(9235139336839550049)
XLA Ops:
  0.7 1.3 %compare_bitcast_fusion = (pred[1024]{0:T(1024)(128)(4,1)}, s32[8,128]{1,0:T(8,128)S(1)}) fusion(s32[8,128]{1,0:T(8,128)} %param.22), kind=kLoop, calls=%fused_computation.114 | loop fusion | flops 3072 | bytes 9216 | tf_op jit(solution)/shard_map/eq | solution.py:156
  1.9 1.3 %fusion.55 = (s32[]{:T(128)}, s32[]{:T(128)}) fusion(s32[8,128]{1,0:T(8,128)} %param.22), kind=kLoop, calls=%fused_computation.135 | loop fusion | flops 4094 | bytes 4104 | tf_op jit(solution)/shard_map/reduce_sum | solution.py:128
  3.3 0.3 reduce-window.25
  3.8 7.6 %scatter_custom_fusion = s32[1024]{0:T(1024)S(1)} fusion(s32[1024]{0:T(1024)S(1)} %bitcast.114, s32[1024]{0:T(1024)S(1)} %broadcast.484, s32[]{:T(128)} %constant.182.clone.1), kind=kCustom, calls=%fused_computation.118 | custom fusion | flops 1024 | bytes 4100 | tf_op jit(solution)/shard_map/scatter-add | solution.py:129
  11.5 0.3 reduce-window.29
  12.0 0.7 compare_and_fusion.1
  12.7 0.7 broadcast_clamp_fusion
  13.4 0.7 compare_select_fusion.1
  14.1 4.5 %gather_fusion.1 = f32[1024]{0:T(1024)S(1)} fusion(f32[1024]{0:T(1024)S(1)} %bitcast.99, s32[1024]{0:T(1024)S(1)} %broadcast_clamp_fusion.1), kind=kCustom, calls=%fused_computation.3 | custom fusion | bytes 12288 | tf_op jit(solution)/shard_map/jit(_take)/gather | solution.py:134
  18.6 0.2 copy.49
  18.9 0.2 copy.46
  19.2 0.2 copy.44
  19.4 2.8 %gather_fusion = f32[1024,28]{1,0:T(8,128)S(1)} fusion(f32[28,1024]{0,1:T(8,128)S(1)} %copy.44, s32[1024]{0:T(1024)S(1)} %broadcast_clamp_fusion.1), kind=kCustom, calls=%fused_computation.2 | custom fusion | bytes 233472 | tf_op jit(solution)/shard_map/jit(_take)/gather | solution.py:132
  22.2 0.2 copy.45
  22.4 0.2 select_bitcast_fusion.1
  22.6 2.8 %gather_fusion.4 = f32[1024,4]{1,0:T(8,128)S(1)} fusion(f32[4,1024]{0,1:T(8,128)S(1)} %bitcast.102, s32[1024]{0:T(1024)S(1)} %broadcast_clamp_fusion), kind=kCustom, calls=%fused_computation.clone | custom fusion | bytes 36864 | tf_op jit(solution)/shard_map/jit(_take)/gather | solution.py:133
  25.5 0.2 select_bitcast_fusion
  25.8 1.0 %and_select_fusion = f32[1,1024]{0,1:T(8,128)S(1)} fusion(f32[1,1024]{0,1:T(8,128)S(1)} %copy.49, s32[1,1024]{0,1:T(8,128)S(1)} %copy.46, s32[]{:T(128)} %get-tuple-element.28), kind=kLoop, calls=%fused_computation.47 | loop fusion | flops 20480 | bytes 12292 | tf_op jit(solution)/shard_map/jit(_take)/select_n | solution.py:134
  26.8 0.3 pad_maximum_fusion
  27.2 4.1 %collective-permute-start = (f32[33,512]{0,1:T(8,128)S(1)}, f32[33,512]{0,1:T(8,128)S(1)}, u32[]{:S(2)}, u32[]{:S(2)}) collective-permute-start(f32[33,512]{0,1:T(8,128)S(1)} %slice.142), channel_id=1, source_target_pairs={{8,0},{12,4},{0,8},{4,12},{9,1},{13,5},{1,9},{5,13},{10,2},{14,6},... | collective-permute-start | bytes 202760 | tf_op jit(solution)/shard_map/ppermute | solution.py:42
  31.4 0.2 fusion.14
  31.6 0.2 convolution_multiply_fusion.5
  31.9 0.2 fusion.12
  32.2 1.6 %collective-permute-start.2 = (f32[4,8,1]{2,1,0:T(8,128)S(1)}, f32[4,8,1]{2,1,0:T(8,128)S(1)}, u32[]{:S(2)}, u32[]{:S(2)}) collective-permute-start(f32[4,8,1]{2,1,0:T(8,128)S(1)} %get-tuple-element.45), channel_id=1, source_target_pairs={{0,4},{4,8},{8,12},{12,0},{1,5},{5,9},{9,13},{13,1},{2,6},{6,10},{... | collective-permute-start | bytes 392 | tf_op jit(solution)/shard_map/ppermute | solution.py:33
  33.8 2.2 %collective-permute-start.3 = (f32[4,8,1]{2,1,0:T(8,128)S(1)}, f32[4,8,1]{2,1,0:T(8,128)S(1)}, u32[]{:S(2)}, u32[]{:S(2)}) collective-permute-start(f32[4,8,1]{2,1,0:T(8,128)S(1)} %get-tuple-element.46), channel_id=1, source_target_pairs={{4,0},{8,4},{12,8},{0,12},{5,1},{9,5},{13,9},{1,13},{6,2},{10,6},{... | collective-permute-start | bytes 392 | tf_op jit(solution)/shard_map/ppermute | solution.py:34
  36.1 0.7 compare_select_fusion.6
  36.7 0.7 iota_compare_fusion.2
  37.4 1.1 %compare_and_fusion.2 = pred[512]{0:T(512)(128)(4,1)} fusion(s32[]{:T(128)} %get-tuple-element.27), kind=kLoop, calls=%fused_computation.131 | loop fusion | flops 4096 | bytes 516 | tf_op jit(solution)/shard_map/jit(_take)/and | solution.py:151
  38.5 0.3 reduce-window.37
  39.0 0.7 fusion.50
  39.7 0.7 compare_and_fusion
  40.4 0.6 compare_convert_fusion.1
  41.0 0.6 pad_clamp_fusion
  41.6 0.7 fusion.43
  42.2 1.5 %collective-permute-done = f32[33,512]{0,1:T(8,128)S(1)} collective-permute-done((f32[33,512]{0,1:T(8,128)S(1)}, f32[33,512]{0,1:T(8,128)S(1)}, u32[]{:S(2)}, u32[]{:S(2)}) %collective-permute-start) | collective-permute-done | bytes 67616 | tf_op jit(solution)/shard_map/ppermute | solution.py:42
  43.8 1.0 %gather_fusion.2 = f32[512,33]{1,0:T(8,128)S(1)} fusion(f32[33,512]{0,1:T(8,128)S(1)} %collective-permute-done, s32[1024]{0:T(1024)S(1)} %pad_clamp_fusion.1), kind=kCustom, calls=%fused_computation.4 | custom fusion | bytes 137216 | tf_op jit(solution)/shard_map/jit(_take)/gather | solution.py:143
  44.8 0.2 slice_select_fusion
  45.0 0.2 slice_reduce_fusion
  45.4 1.8 %divide_exponential_fusion = f32[4,512,224]{1,2,0:T(8,128)S(1)} fusion(f32[512]{0:T(512)S(1)} %slice_reduce_fusion, f32[7,4,512]{2,1,0:T(4,128)S(1)} %reshape.370, f32[7,224]{1,0:T(8,128)S(1)} %copy-done), kind=kOutput, calls=%fused_computation.16 | convolution fusion | flops 39452672 | bytes 1900672 | tf_op jit(solution)/shard_map/skc,sg->kgc/dot_general | solution.py:63
  47.3 1.4 %fusion = f32[4,224,512]{2,1,0:T(8,128)S(1)} fusion(f32[4,512,224]{1,2,0:T(8,128)S(1)} %divide_exponential_fusion), kind=kOutput, calls=%fused_computation.9 | output fusion | flops 1376256 | bytes 3670016 | tf_op jit(solution)/shard_map/jit(cumprod)/reduce_window | solution.py:65
  48.8 1.2 %copy-done.2 = f32[4,224,512]{2,1,0:T(8,128)} copy-done((f32[4,224,512]{2,1,0:T(8,128)}, f32[4,224,512]{2,1,0:T(8,128)S(1)}, u32[]{:S(2)}) %copy-start.2) | copy-done | bytes 1835032
  50.0 12.2 %all_gather.3 = f32[2,224,512]{2,1,0:T(8,128)S(1)} all-gather(f32[1,224,512]{2,1,0:T(8,128)S(1)} %slice.146), channel_id=1, replica_groups=mesh['grp'=2,'wide'=4,'lev'=2,'sub'=2] {'lev'}, dimensions={0}, use_global_device_ids=true | all-gather | bytes 1376256 | tf_op jit(solution)/shard_map/all_gather | solution.py:17
  62.3 1.3 %slice-done = f32[3,224,512]{2,1,0:T(8,128)S(1)} async-done(((f32[4,224,512]{2,1,0:T(8,128)}), f32[3,224,512]{2,1,0:T(8,128)S(1)}, s32[]{:S(2)}) %slice-start) | async-done | bytes 1376280 | tf_op jit(solution)/shard_map/slice | solution.py:67
  63.6 2.8 %fusion.3 = f32[1,4,512]{2,0,1:T(1,128)S(1)} fusion(f32[224,1,1]{0,1,2:T(1,128)S(1)} %bitcast.115, f32[4,512,224]{1,2,0:T(8,128)} %copy-done.3, f32[3,224,512]{2,1,0:T(8,128)S(1)} %slice-done, f32[224,512]{1,0:T(8,128)S(1)} %get-tuple-element.26, f32[512]{0:T(512)S(1)} %copy-done.18), kind=kOutput, calls=%fused_computation.12 | convolution fusion | flops 7340032 | bytes 3681152 | tf_op jit(solution)/shard_map/kgc,g->kc/dot_general | solution.py:74
  66.4 0.1 copy.55
  66.5 0.1 slice_divide_fusion
  66.8 1.0 %gather_fusion.3 = f32[512,4]{1,0:T(8,128)S(1)} fusion(f32[4,512]{0,1:T(8,128)S(1)} %slice_divide_fusion, s32[1024]{0:T(1024)S(1)} %copy-done.16), kind=kCustom, calls=%fused_computation.5 | custom fusion | bytes 18432 | tf_op jit(solution)/shard_map/jit(_take)/gather | solution.py:151
  67.9 0.1 select_bitcast_fusion.2
  68.0 4.5 %collective-permute-start.1 = (f32[4,512]{0,1:T(8,128)S(1)}, f32[4,512]{0,1:T(8,128)S(1)}, u32[]{:S(2)}, u32[]{:S(2)}) collective-permute-start(f32[4,512]{0,1:T(8,128)S(1)} %select_bitcast_fusion.2), channel_id=1, source_target_pairs={{8,0},{12,4},{0,8},{4,12},{9,1},{13,5},{1,9},{5,13},{10,2},{14,6},... | collective-permute-start | bytes 24584 | tf_op jit(solution)/shard_map/ppermute | solution.py:42
  72.6 0.5 collective-permute-start.5
  73.1 10.7 %collective-permute-done.1 = f32[4,512]{0,1:T(8,128)S(1)} collective-permute-done((f32[4,512]{0,1:T(8,128)S(1)}, f32[4,512]{0,1:T(8,128)S(1)}, u32[]{:S(2)}, u32[]{:S(2)}) %collective-permute-start.1) | collective-permute-done | bytes 8224 | tf_op jit(solution)/shard_map/ppermute | solution.py:42
  83.8 2.8 %gather_fusion.5 = f32[1024,4]{1,0:T(8,128)S(1)} fusion(f32[4,1024]{0,1:T(8,128)S(1)} %pad_maximum_fusion.1, s32[1024]{0:T(1024)S(1)} %copy-done.15), kind=kCustom, calls=%fused_computation.1.clone | custom fusion | bytes 36864 | tf_op jit(solution)/shard_map/jit(_take)/gather | solution.py:155
  86.6 0.3 bitcast_select_fusion
  87.0 0.2 copy.58
  87.3 0.2 convolution_multiply_fusion.2
  87.5 0.1 fusion.10
  87.7 0.2 convolution_multiply_fusion.1
  87.9 0.2 fusion.9
  88.1 3.8 %collective-permute-start.7 = (f32[4,8,1]{2,1,0:T(8,128)S(1)}, f32[4,8,1]{2,1,0:T(8,128)S(1)}, u32[]{:S(2)}, u32[]{:S(2)}) collective-permute-start(f32[4,8,1]{2,1,0:T(8,128)S(1)} %get-tuple-element.42), channel_id=1, source_target_pairs={{4,0},{8,4},{12,8},{0,12},{5,1},{9,5},{13,9},{1,13},{6,2},{10,6},{... | collective-permute-start | bytes 392 | tf_op jit(solution)/shard_map/ppermute | solution.py:34
  92.0 1.7 %collective-permute-done.6 = f32[4,8,1]{2,1,0:T(8,128)S(1)} collective-permute-done((f32[4,8,1]{2,1,0:T(8,128)S(1)}, f32[4,8,1]{2,1,0:T(8,128)S(1)}, u32[]{:S(2)}, u32[]{:S(2)}) %collective-permute-start.6) | collective-permute-done | bytes 160 | tf_op jit(solution)/shard_map/ppermute | solution.py:33
  93.9 0.5 collective-permute-start.9
  94.4 0.6 collective-permute-done.8
  95.0 0.2 collective-permute-done.9
  95.2 0.7 fusion.27
  (112 shorter events, 2.0 us)
Async XLA Ops:
  0.6 44.8 %copy-start = (f32[7,224]{1,0:T(8,128)S(1)}, f32[7,224]{1,0:T(8,128)}, u32[]{:S(2)}) copy-start(f32[7,224]{1,0:T(8,128)} %param.23) | copy-start | bytes 18820
  0.6 13.4 %copy-start.1 = (f32[8,128]{1,0:T(8,128)S(1)}, f32[8,128]{1,0:T(8,128)}, u32[]{:S(2)}) copy-start(f32[8,128]{1,0:T(8,128)} %param.21) | copy-start | bytes 12292
  14.1 5.0 %copy-start.8 = (f32[7,4,8,128]{3,2,1,0:T(8,128)S(1)}, f32[7,4,8,128]{3,2,1,0:T(8,128)}, u32[]{:S(2)}) copy-start(f32[7,4,8,128]{3,2,1,0:T(8,128)} %param.19) | copy-start | bytes 344068
  18.6 3.6 %copy-start.11 = (f32[4,8,128]{2,1,0:T(8,128)S(1)}, f32[4,8,128]{2,1,0:T(8,128)}, u32[]{:S(2)}) copy-start(f32[4,8,128]{2,1,0:T(8,128)} %param.20) | copy-start | bytes 49156
  25.7 5.6 %copy-start.19 = (f32[8,128]{1,0:T(8,128)S(1)}, f32[8,128]{1,0:T(8,128)}, u32[]{:S(2)}) copy-start(f32[8,128]{1,0:T(8,128)} %param.18) | copy-start | bytes 12292
  25.7 5.6 %copy-start.32 = (f32[128]{0:T(128)S(1)}, f32[128]{0:T(128)}, u32[]{:S(2)}) copy-start(f32[128]{0:T(128)} %constant.198.clone) | copy-start | bytes 1540
  25.7 5.6 %copy-start.33 = (f32[8]{0:T(128)S(1)}, f32[8]{0:T(128)}, u32[]{:S(2)}) copy-start(f32[8]{0:T(128)} %constant.199.clone) | copy-start | bytes 100
  25.7 5.7 %copy-start.4 = (f32[128,128,1]{1,0,2:T(8,128)S(1)}, f32[128,128,1]{1,0,2:T(8,128)}, u32[]{:S(2)}) copy-start(f32[128,128,1]{1,0,2:T(8,128)} %constant.207) | copy-start | bytes 196612
  25.7 5.7 %copy-start.5 = (f32[4,8,128]{2,1,0:T(8,128)S(1)}, f32[4,8,128]{2,1,0:T(8,128)}, u32[]{:S(2)}) copy-start(f32[4,8,128]{2,1,0:T(8,128)} %param.17) | copy-start | bytes 49156
  25.7 5.9 %copy-start.22 = (f32[8]{0:T(128)S(1)}, f32[8]{0:T(128)}, u32[]{:S(2)}) copy-start(f32[8]{0:T(128)} %constant.205) | copy-start | bytes 100
  25.7 6.1 %copy-start.13 = (f32[8,8,1]{1,0,2:T(8,128)S(1)}, f32[8,8,1]{1,0,2:T(8,128)}, u32[]{:S(2)}) copy-start(f32[8,8,1]{1,0,2:T(8,128)} %constant.208) | copy-start | bytes 772
  25.8 6.2 %copy-start.34 = (f32[128]{0:T(128)S(1)}, f32[128]{0:T(128)}, u32[]{:S(2)}) copy-start(f32[128]{0:T(128)} %constant.206) | copy-start | bytes 1540
  26.8 11.7 %copy-start.10 = (s32[8,128]{1,0:T(8,128)S(1)}, s32[8,128]{1,0:T(8,128)}, u32[]{:S(2)}) copy-start(s32[8,128]{1,0:T(8,128)} %param.22) | copy-start | bytes 12292
  27.2 16.6 %collective-permute-start = (f32[33,512]{0,1:T(8,128)S(1)}, f32[33,512]{0,1:T(8,128)S(1)}, u32[]{:S(2)}, u32[]{:S(2)}) collective-permute-start(f32[33,512]{0,1:T(8,128)S(1)} %slice.142), channel_id=1, source_target_pairs={{8,0},{12,4},{0,8},{4,12},{9,1},{13,5},{1,9},{5,13},{10,2},{14,6},... | collective-permute-start | bytes 202760 | tf_op jit(solution)/shard_map/ppermute | solution.py:42
  32.2 9.3 %collective-permute-start.2 = (f32[4,8,1]{2,1,0:T(8,128)S(1)}, f32[4,8,1]{2,1,0:T(8,128)S(1)}, u32[]{:S(2)}, u32[]{:S(2)}) collective-permute-start(f32[4,8,1]{2,1,0:T(8,128)S(1)} %get-tuple-element.45), channel_id=1, source_target_pairs={{0,4},{4,8},{8,12},{12,0},{1,5},{5,9},{9,13},{13,1},{2,6},{6,10},{... | collective-permute-start | bytes 392 | tf_op jit(solution)/shard_map/ppermute | solution.py:33
  33.8 7.7 %collective-permute-start.3 = (f32[4,8,1]{2,1,0:T(8,128)S(1)}, f32[4,8,1]{2,1,0:T(8,128)S(1)}, u32[]{:S(2)}, u32[]{:S(2)}) collective-permute-start(f32[4,8,1]{2,1,0:T(8,128)S(1)} %get-tuple-element.46), channel_id=1, source_target_pairs={{4,0},{8,4},{12,8},{0,12},{5,1},{9,5},{13,9},{1,13},{6,2},{10,6},{... | collective-permute-start | bytes 392 | tf_op jit(solution)/shard_map/ppermute | solution.py:34
  40.4 6.9 %copy-start.26 = (f32[128]{0:T(128)}, f32[128]{0:T(128)S(1)}, u32[]{:S(2)}) copy-start(f32[128]{0:T(128)S(1)} %get-tuple-element.55) | copy-start | bytes 1540
  40.4 6.9 %copy-start.28 = (f32[128]{0:T(128)}, f32[128]{0:T(128)S(1)}, u32[]{:S(2)}) copy-start(f32[128]{0:T(128)S(1)} %get-tuple-element.56) | copy-start | bytes 1540
  45.2 2.0 %copy-start.17 = (f32[512]{0:T(512)}, f32[512]{0:T(512)S(1)}, u32[]{:S(2)}) copy-start(f32[512]{0:T(512)S(1)} %slice_reduce_fusion) | copy-start | bytes 6148
  47.3 1.5 %copy-start.3 = (f32[4,512,224]{1,2,0:T(8,128)}, f32[4,512,224]{1,2,0:T(8,128)S(1)}, u32[]{:S(2)}) copy-start(f32[4,512,224]{1,2,0:T(8,128)S(1)} %divide_exponential_fusion) | copy-start | bytes 5505028
  48.7 1.2 %copy-start.2 = (f32[4,224,512]{2,1,0:T(8,128)}, f32[4,224,512]{2,1,0:T(8,128)S(1)}, u32[]{:S(2)}) copy-start(f32[4,224,512]{2,1,0:T(8,128)S(1)} %fusion) | copy-start | bytes 5505028
  62.2 1.3 %slice-start = ((f32[4,224,512]{2,1,0:T(8,128)}), f32[3,224,512]{2,1,0:T(8,128)S(1)}, s32[]{:S(2)}) async-start(f32[4,224,512]{2,1,0:T(8,128)} %copy-done.2), calls=%async_computation | async-start | bytes 2752512 | tf_op jit(solution)/shard_map/slice | solution.py:67
  62.2 1.3 %copy-start.18 = (f32[512]{0:T(512)S(1)}, f32[512]{0:T(512)}, u32[]{:S(2)}) copy-start(f32[512]{0:T(512)} %copy-done.17) | copy-start | bytes 6148
  62.2 1.3 %copy-start.30 = (f32[224]{0:T(256)S(1)}, f32[224]{0:T(256)}, u32[]{:S(2)}) copy-start(f32[224]{0:T(256)} %param.24) | copy-start | bytes 2692
  63.6 3.1 %copy-start.16 = (s32[1024]{0:T(1024)S(1)}, s32[1024]{0:T(1024)}, u32[]{:S(2)}) copy-start(s32[1024]{0:T(1024)} %pad_clamp_fusion) | copy-start | bytes 12292
  63.6 4.2 %copy-start.31 = (pred[512]{0:T(512)(128)(4,1)S(1)}, pred[512]{0:T(512)(128)(4,1)}, u32[]{:S(2)}) copy-start(pred[512]{0:T(512)(128)(4,1)} %compare_and_fusion.2) | copy-start | bytes 1540
  63.6 8.9 %copy-start.9 = (f32[4,8,128]{2,1,0:T(8,128)S(1)}, f32[4,8,128]{2,1,0:T(8,128)}, u32[]{:S(2)}) copy-start(f32[4,8,128]{2,1,0:T(8,128)} %fusion.43) | copy-start | bytes 49156
  66.4 17.4 %copy-start.15 = (s32[1024]{0:T(1024)S(1)}, s32[1024]{0:T(1024)}, u32[]{:S(2)}) copy-start(s32[1024]{0:T(1024)} %fusion.50) | copy-start | bytes 12292
  66.4 20.3 %copy-start.20 = (pred[1024]{0:T(1024)(128)(4,1)S(1)}, pred[1024]{0:T(1024)(128)(4,1)}, u32[]{:S(2)}) copy-start(pred[1024]{0:T(1024)(128)(4,1)} %get-tuple-element.49) | copy-start | bytes 3076
  66.4 20.2 %copy-start.21 = (pred[1024]{0:T(1024)(128)(4,1)S(1)}, pred[1024]{0:T(1024)(128)(4,1)}, u32[]{:S(2)}) copy-start(pred[1024]{0:T(1024)(128)(4,1)} %compare_and_fusion) | copy-start | bytes 3076
  66.7 20.5 %copy-start.6 = (f32[4,8,128]{2,1,0:T(8,128)S(1)}, f32[4,8,128]{2,1,0:T(8,128)}, u32[]{:S(2)}) copy-start(f32[4,8,128]{2,1,0:T(8,128)} %param.17) | copy-start | bytes 49156
  66.7 20.5 %copy-start.12 = (f32[8,128]{1,0:T(8,128)S(1)}, f32[8,128]{1,0:T(8,128)}, u32[]{:S(2)}) copy-start(f32[8,128]{1,0:T(8,128)} %constant.203) | copy-start | bytes 12292
  66.7 20.5 %copy-start.24 = (f32[8]{0:T(128)S(1)}, f32[8]{0:T(128)}, u32[]{:S(2)}) copy-start(f32[8]{0:T(128)} %get-tuple-element.57) | copy-start | bytes 100
  66.7 20.5 %copy-start.25 = (f32[8]{0:T(128)S(1)}, f32[8]{0:T(128)}, u32[]{:S(2)}) copy-start(f32[8]{0:T(128)} %get-tuple-element.58) | copy-start | bytes 100
  66.7 20.8 %copy-start.14 = (f32[8,8,1]{1,0,2:T(8,128)S(1)}, f32[8,8,1]{1,0,2:T(8,128)}, u32[]{:S(2)}) copy-start(f32[8,8,1]{1,0,2:T(8,128)} %constant.208) | copy-start | bytes 772
  66.8 20.9 %copy-start.23 = (f32[8]{0:T(128)S(1)}, f32[8]{0:T(128)}, u32[]{:S(2)}) copy-start(f32[8]{0:T(128)} %constant.205) | copy-start | bytes 100
  67.8 20.0 %copy-start.35 = (f32[128]{0:T(128)S(1)}, f32[128]{0:T(128)}, u32[]{:S(2)}) copy-start(f32[128]{0:T(128)} %constant.206) | copy-start | bytes 1540
  67.8 25.9 %copy-start.27 = (f32[128]{0:T(128)S(1)}, f32[128]{0:T(128)}, u32[]{:S(2)}) copy-start(f32[128]{0:T(128)} %copy-done.26) | copy-start | bytes 1540
  67.8 25.9 %copy-start.29 = (f32[128]{0:T(128)S(1)}, f32[128]{0:T(128)}, u32[]{:S(2)}) copy-start(f32[128]{0:T(128)} %copy-done.28) | copy-start | bytes 1540
  68.0 15.7 %collective-permute-start.1 = (f32[4,512]{0,1:T(8,128)S(1)}, f32[4,512]{0,1:T(8,128)S(1)}, u32[]{:S(2)}, u32[]{:S(2)}) collective-permute-start(f32[4,512]{0,1:T(8,128)S(1)} %select_bitcast_fusion.2), channel_id=1, source_target_pairs={{8,0},{12,4},{0,8},{4,12},{9,1},{13,5},{1,9},{5,13},{10,2},{14,6},... | collective-permute-start | bytes 24584 | tf_op jit(solution)/shard_map/ppermute | solution.py:42
  72.5 14.7 %collective-permute-start.4 = (f32[4,1,128]{2,1,0:T(1,128)S(1)}, f32[4,1,128]{2,1,0:T(1,128)S(1)}, u32[]{:S(2)}, u32[]{:S(2)}) collective-permute-start(f32[4,1,128]{2,1,0:T(1,128)S(1)} %get-tuple-element.43), channel_id=1, source_target_pairs={{0,1},{1,0},{2,3},{3,2},{4,5},{5,4},{6,7},{7,6},{8,9},{9,8},{10,11... | collective-permute-start | bytes 6152 | tf_op jit(solution)/shard_map/ppermute | solution.py:33
  72.6 14.6 %collective-permute-start.5 = (f32[4,1,128]{2,1,0:T(1,128)S(1)}, f32[4,1,128]{2,1,0:T(1,128)S(1)}, u32[]{:S(2)}, u32[]{:S(2)}) collective-permute-start(f32[4,1,128]{2,1,0:T(1,128)S(1)} %get-tuple-element.44), channel_id=1, source_target_pairs={{1,0},{0,1},{3,2},{2,3},{5,4},{4,5},{7,6},{6,7},{9,8},{8,9},{11,10... | collective-permute-start | bytes 6152 | tf_op jit(solution)/shard_map/ppermute | solution.py:34
  87.2 8.7 %copy-start.7 = (f32[4,8,128]{2,1,0:T(8,128)}, f32[4,8,128]{2,1,0:T(8,128)S(1)}, u32[]{:S(2)}) copy-start(f32[4,8,128]{2,1,0:T(8,128)S(1)} %copy.58) | copy-start | bytes 49156
  88.1 5.5 %collective-permute-start.6 = (f32[4,8,1]{2,1,0:T(8,128)S(1)}, f32[4,8,1]{2,1,0:T(8,128)S(1)}, u32[]{:S(2)}, u32[]{:S(2)}) collective-permute-start(f32[4,8,1]{2,1,0:T(8,128)S(1)} %get-tuple-element.41), channel_id=1, source_target_pairs={{0,4},{4,8},{8,12},{12,0},{1,5},{5,9},{9,13},{13,1},{2,6},{6,10},{... | collective-permute-start | bytes 392 | tf_op jit(solution)/shard_map/ppermute | solution.py:33
  88.1 5.5 %collective-permute-start.7 = (f32[4,8,1]{2,1,0:T(8,128)S(1)}, f32[4,8,1]{2,1,0:T(8,128)S(1)}, u32[]{:S(2)}, u32[]{:S(2)}) collective-permute-start(f32[4,8,1]{2,1,0:T(8,128)S(1)} %get-tuple-element.42), channel_id=1, source_target_pairs={{4,0},{8,4},{12,8},{0,12},{5,1},{9,5},{13,9},{1,13},{6,2},{10,6},{... | collective-permute-start | bytes 392 | tf_op jit(solution)/shard_map/ppermute | solution.py:34
  93.8 1.2 %collective-permute-start.8 = (f32[4,1,128]{2,1,0:T(1,128)S(1)}, f32[4,1,128]{2,1,0:T(1,128)S(1)}, u32[]{:S(2)}, u32[]{:S(2)}) collective-permute-start(f32[4,1,128]{2,1,0:T(1,128)S(1)} %get-tuple-element.39), channel_id=1, source_target_pairs={{0,1},{1,0},{2,3},{3,2},{4,5},{5,4},{6,7},{7,6},{8,9},{9,8},{10,11... | collective-permute-start | bytes 6152 | tf_op jit(solution)/shard_map/ppermute | solution.py:33
  93.9 1.3 %collective-permute-start.9 = (f32[4,1,128]{2,1,0:T(1,128)S(1)}, f32[4,1,128]{2,1,0:T(1,128)S(1)}, u32[]{:S(2)}, u32[]{:S(2)}) collective-permute-start(f32[4,1,128]{2,1,0:T(1,128)S(1)} %get-tuple-element.40), channel_id=1, source_target_pairs={{1,0},{0,1},{3,2},{2,3},{5,4},{4,5},{7,6},{6,7},{9,8},{8,9},{11,10... | collective-permute-start | bytes 6152 | tf_op jit(solution)/shard_map/ppermute | solution.py:34
where the time goes:
time: 96.2 us; the launch traced here: 95.9 us
  other arithmetic  23.9 us (25%)
  local copies, waits for them, and re-layouts  20.2 us (21%)
  starting transfers between devices  17.4 us (18%)
  waiting for transfers between devices  14.7 us (15%)
  blocking collectives  12.2 us (13%)
  matrix products  6 us (6%)
  between operations  1.43 us (1%)
    all_gather x1, blocking collectives, carried_in(): gathered = lax.all_gather(part, axis)  12.2 us
    ppermute x2, waiting for transfers between devices, from_behind(): return lax.ppermute(block, axis, route)  12.2 us
    ppermute x2, starting transfers between devices, from_behind(): return lax.ppermute(block, axis, route)  8.59 us
    scatter-add x1, other arithmetic, shards(): jnp.nonzero(flat_lit, size=columns, fill_value=0)[0].astype(jnp.int32)  7.62 us
    ppermute x4, starting transfers between devices, padded_2(): after = lax.ppermute(initial, axis, down)  7.06 us
    gather x2, local copies, waits for them, and re-layouts, shards(): jnp.take(zenith_flat, own_index)[None, :]  4.75 us
    gather x1, local copies, waits for them, and re-layouts, shards(): jnp.take(amount_flat, own_index, axis=1)  2.81 us
    gather x1, local copies, waits for them, and re-layouts, shards(): jnp.take(layer_flat, own_index, axis=1)  2.81 us
  transfers between devices with their start and end apart: 10, of which 5 were waited for; matrix products, arithmetic and copies ran while one was open for 11% of the time, Pallas kernels for 0%

commit v1 on v0

v1 whole, which is shorter than its diff:
```python
import math

import jax
import jax.numpy as jnp
import numpy as np
from jax import lax
from jax.experimental import pallas as pl
from jax.experimental.pallas import tpu as pltpu
from jax.sharding import PartitionSpec as P

time_step = 0.004
points = 4
log2e = 1.4426950408889634
gll_weights = (1.0 / 6.0, 5.0 / 6.0, 5.0 / 6.0, 1.0 / 6.0)
mass_points = (1.0 / 3.0, 5.0 / 6.0, 5.0 / 6.0, 1.0 / 3.0)


def derivative_table():
    root_five = math.sqrt(5.0)
    outer_big = (5.0 + 5.0 * root_five) / 4.0
    outer_small = (5.0 * root_five - 5.0) / 4.0
    inner_big = (1.0 + root_five) / 4.0
    inner_mid = root_five / 2.0
    inner_small = (root_five - 1.0) / 4.0
    return np.array(
        [
            [-3.0, outer_big, -outer_small, 0.5],
            [-inner_big, 0.0, inner_mid, -inner_small],
            [inner_small, -inner_mid, 0.0, inner_big],
            [-0.5, outer_small, -outer_big, 3.0],
        ]
    )


table = derivative_table()


def by_node(node, values):
    out = jnp.full(node.shape, values[3], jnp.float32)
    for i in (2, 1, 0):
        out = jnp.where(node == i, jnp.float32(values[i]), out)
    return out


class Stencil:
    def __init__(self, rows, width):
        self.shape = (rows, width)
        self.row = lax.broadcasted_iota(jnp.int32, (rows, width), 0)
        self.lane = lax.broadcasted_iota(jnp.int32, (rows, width), 1)
        node_y, node_x = self.row % points, self.lane % points
        self.weight_x = by_node(node_x, gll_weights)
        self.weight_y = by_node(node_y, gll_weights)
        self.coefs = {}
        for name, matrix in (("d", table), ("t", table.T)):
            for axis, node in ((0, node_y), (1, node_x)):
                terms = []
                for step in range(-3, 4):
                    values = [
                        matrix[i, i + step] if 0 <= i + step < points else 0.0
                        for i in range(points)
                    ]
                    terms.append(by_node(node, values))
                self.coefs[name, axis] = terms
        self.inv_mass = by_node(node_y, [1.0 / m for m in mass_points]) * by_node(
            node_x, [1.0 / m for m in mass_points]
        )
        self.first_x = (node_x == 0).astype(jnp.float32)
        self.last_x = (node_x == points - 1).astype(jnp.float32)
        self.first_y = (node_y == 0).astype(jnp.float32)
        self.last_y = (node_y == points - 1).astype(jnp.float32)

    def apply(self, name, axis, field):
        size = self.shape[axis]
        out = None
        for step, coef in zip(range(-3, 4), self.coefs[name, axis]):
            if step == 0 and name == "d":
                moved = field
            else:
                moved = pltpu.roll(field, (-step) % size, field.ndim - 2 + axis)
            term = coef * moved
            out = term if out is None else out + term
        return out

    def shifted(self, field, axis, step):
        size = self.shape[axis]
        index = self.row if axis == 0 else self.lane
        moved = pltpu.roll(field, step % size, field.ndim - 2 + axis)
        if axis == 0:
            other = jnp.concatenate([moved[:, 1:], moved[:, :1]], axis=1)
        else:
            other = jnp.concatenate([moved[:, :, 1:], moved[:, :, :1]], axis=2)
        edge = 0 if step == 1 else size - 1
        return jnp.where(index == edge, other, moved)

    def tendency(self, field, kappa):
        flux_x = kappa * self.weight_x * self.apply("d", 1, field)
        flux_y = kappa * self.weight_y * self.apply("d", 0, field)
        r = -self.weight_y * self.apply("t", 1, flux_x) - self.weight_x * self.apply("t", 0, flux_y)
        r = (
            r
            + self.first_x * self.shifted(r, 1, 1)
            + self.last_x * self.shifted(r, 1, -1)
        )
        r = (
            r
            + self.first_y * self.shifted(r, 0, 1)
            + self.last_y * self.shifted(r, 0, -1)
        )
        return r * self.inv_mass


def split(value, pieces):
    out = []
    for _ in range(pieces):
        high = value.astype(jnp.bfloat16)
        out.append(high)
        value = value - high.astype(jnp.float32)
    return out


def radiate_kernel(
    absorber, upper, zenith, lit, thickness, coef, weight, heat, spread, left
):
    species, levels, rows, width = absorber.shape
    terms = coef.shape[1]
    group = species * rows
    depth = 256
    c_pieces = split(coef[...], 2)
    w_pieces = split(jnp.log2(weight[...]), 3)
    lane = lax.broadcasted_iota(jnp.int32, (rows, depth), 1)
    row = lax.broadcasted_iota(jnp.int32, (rows, depth), 0)
    ones_at = 4 * group
    stack = jnp.concatenate(
        [p.astype(jnp.float32) for p in c_pieces] + [p.astype(jnp.float32) for p in w_pieces],
        axis=0,
    )
    count = stack.shape[0]
    pick_row = lax.broadcasted_iota(jnp.int32, (count, depth), 0)
    pick_lane = lax.broadcasted_iota(jnp.int32, (count, depth), 1)
    kind = pick_lane // group
    wanted = jnp.where(kind == 3, species, 0) + (pick_lane % group) // rows
    wanted = jnp.where(kind >= 4, 2 * species + pick_lane - ones_at, wanted)
    pick = (pick_row == wanted).astype(jnp.bfloat16)
    spread[...] = lax.dot_general(
        stack.astype(jnp.bfloat16),
        pick,
        (((0,), (0,)), ((), ())),
        preferred_element_type=jnp.float32,
    )
    mask = ((lane % rows == row) | (lane >= ones_at)).astype(jnp.float32)
    for g in range(0, terms, 2):
        pair = [jnp.broadcast_to(spread[pl.ds(g + i, 1), :], (rows, depth)) * mask for i in (0, 1)]
        left[pl.ds(g * rows, 2 * rows), :] = jnp.concatenate(pair, axis=0).astype(jnp.bfloat16)

    scale = -log2e / zenith[...]
    total = [upper[s] for s in range(species)]
    blocks = []
    for k in range(levels + 1):
        if k:
            total = [total[s] + absorber[s, k - 1] for s in range(species)]
        value = jnp.concatenate([t * scale for t in total], axis=0)
        hi, mid, lo = (p.astype(jnp.float32) for p in split(value, 3))
        ones = jnp.where(
            lax.broadcasted_iota(jnp.int32, (depth - ones_at, width), 0) < 3, 1.0, 0.0
        )
        blocks.append(jnp.concatenate([hi, mid, lo, hi, ones], axis=0).astype(jnp.bfloat16))
    right = jnp.concatenate(blocks, axis=1)

    chunk = 448
    sums = [jnp.zeros((rows, width), jnp.float32) for _ in range(levels)]
    for start in range(0, terms * rows, chunk):
        out = jnp.exp2(
            jnp.dot(left[pl.ds(start, chunk), :], right, preferred_element_type=jnp.float32)
        )
        for k in range(levels):
            drop = out[:, k * width : (k + 1) * width] - out[:, (k + 1) * width : (k + 2) * width]
            sums[k] = sums[k] + jnp.sum(drop.reshape(chunk // rows, rows, width), axis=0)
    lit_zenith = jnp.where(lit[...] == 1, zenith[...], 0.0)
    for k in range(levels):
        heat[k] = lit_zenith * sums[k] / thickness[k]


def strips(levels):
    return [(i, tile) for i in range(2 * levels + 1) for tile in range(2)]


def pack_kernel(own_state, own_heat, other_state, other_heat, odd_first, even_first):
    levels = own_heat.shape[0]
    rows, width = own_heat.shape[1:]
    edge = 2 * points
    slots = width // edge
    lane = lax.broadcasted_iota(jnp.int32, (rows, width), 1)
    tiles = [(jnp.zeros((rows, width), jnp.float32), jnp.zeros((rows, width), jnp.float32)) for _ in range(own_first_tiles(levels, slots))]
    for j, (i, tile) in enumerate(strips(levels)):
        state, heat = (own_state, own_heat) if tile == 0 else (other_state, other_heat)
        value = state[i] if i <= levels else heat[i - levels - 1]
        n, slot = divmod(j, slots)
        here = lane // edge == slot
        low = pltpu.roll(value, (slot * edge) % width, 1)
        high = pltpu.roll(value, (slot * edge + edge) % width, 1)
        tiles[n] = (jnp.where(here, low, tiles[n][0]), jnp.where(here, high, tiles[n][1]))
    even = lax.axis_index("wide") % 2 == 0
    for n, (low, high) in enumerate(tiles):
        odd_first[n] = jnp.where(even, low, high)
        even_first[n] = jnp.where(even, high, low)


def own_first_tiles(levels, slots):
    return -(-(2 * (2 * levels + 1)) // slots)


def step_kernel(own_state, own_heat, other_state, other_heat, got_one, got_two, out):
    levels = own_heat.shape[0]
    rows, width = own_heat.shape[1:]
    edge = 2 * points
    slots = width // edge
    stencil = Stencil(rows, width)
    even = lax.axis_index("wide") % 2 == 0
    lane = stencil.lane
    halo = {}
    for j, (i, tile) in enumerate(strips(levels)):
        n, slot = divmod(j, slots)
        from_left = jnp.where(even, got_one[n], got_two[n])
        from_right = jnp.where(even, got_two[n], got_one[n])
        after = pltpu.roll(from_right, (-slot * edge) % width, 1)
        before = pltpu.roll(from_left, (-slot * edge - edge) % width, 1)
        value = jnp.where(lane < edge, after, jnp.where(lane >= width - edge, before, 0.0))
        halo[i, tile] = value

    def ring(i):
        parts = []
        for tile in range(2):
            state, heat = (own_state, own_heat) if tile == 0 else (other_state, other_heat)
            main = state[i] if i <= levels else heat[i - levels - 1]
            parts.append(jnp.stack([main, halo[i, tile]], axis=0))
        return jnp.stack(parts, axis=0)

    air = jnp.stack([ring(i) for i in range(levels)], axis=0)
    kappa = ring(levels)[None]
    heat = jnp.stack([ring(levels + 1 + i) for i in range(levels)], axis=0)
    first = air + time_step * (stencil.tendency(air, kappa) + heat)
    new = 0.5 * (air + first + time_step * (stencil.tendency(first, kappa) + heat))
    for k in range(levels):
        out[k] = new[k, 0, 0]


def swap(value, axis, pairs):
    route = [(a, b) for a, b in pairs] + [(b, a) for a, b in pairs]
    return lax.ppermute(value, axis, route)


def shards(
    air_state, diffusivity, absorber, thickness, cos_zenith, sunlit, absorb_coef, solar_weight
):
    levels, rows, width = air_state.shape
    terms = absorb_coef.shape[1]
    tile = lambda n: jax.ShapeDtypeStruct((n, rows, width), jnp.float32)
    big = pltpu.CompilerParams(vmem_limit_bytes=32 * 1024 * 1024)
    own_state = jnp.concatenate([air_state, diffusivity[None]], axis=0)
    other_state = swap(own_state, "sub", [(0, 1)])
    amount = jnp.sum(absorber, axis=1)
    size = lax.axis_size("lev")
    upper = jnp.zeros_like(amount)
    for step in range(1, size):
        upper = upper + lax.ppermute(amount, "lev", [(i, i + step) for i in range(size - step)])
    heat = pl.pallas_call(
        radiate_kernel,
        out_shape=tile(levels),
        scratch_shapes=[
            pltpu.VMEM((terms, 256), jnp.float32),
            pltpu.VMEM((terms * rows, 256), jnp.bfloat16),
        ],
        compiler_params=big,
        name="radiate",
    )(absorber, upper, cos_zenith, sunlit, thickness, absorb_coef, solar_weight[None])
    other_heat = swap(heat, "sub", [(0, 1)])
    tiles = own_first_tiles(levels, width // (2 * points))
    odd_first, even_first = pl.pallas_call(
        pack_kernel, out_shape=(tile(tiles), tile(tiles)), compiler_params=big, name="pack"
    )(own_state, heat, other_state, other_heat)
    wide = lax.axis_size("wide")
    got_one = swap(odd_first, "wide", [(i, (i + 1) % wide) for i in range(1, wide, 2)])
    got_two = swap(even_first, "wide", [(i, i + 1) for i in range(0, wide, 2)])
    new_state = pl.pallas_call(
        step_kernel, out_shape=tile(levels), compiler_params=big, name="step"
    )(own_state, heat, other_state, other_heat, got_one, got_two)
    return (heat, new_state)


def solution(mesh):
    in_specs = (
        P("lev", ("grp", "sub"), "wide"),
        P(("grp", "sub"), "wide"),
        P(None, "lev", ("grp", "sub"), "wide"),
        P("lev", ("grp", "sub"), "wide"),
        P(("grp", "sub"), "wide"),
        P(("grp", "sub"), "wide"),
        P(),
        P(),
    )
    out_specs = (P("lev", ("grp", "sub"), "wide"), P("lev", ("grp", "sub"), "wide"))
    return jax.shard_map(shards, mesh=mesh, in_specs=in_specs, out_specs=out_specs, check_vma=False)
```

time: 96.2 us -> 21 us (0.22)
  other arithmetic: 23.9 us -> 0.96 us
  local copies, waits for them, and re-layouts: 20.2 us -> 0.76 us
  blocking collectives: 12.2 us -> 0 us
  starting transfers between devices: 17.4 us -> 8.59 us
  waiting for transfers between devices: 14.7 us -> 6.41 us
  matrix products: 6 us -> 0 us
  Pallas kernels: 0 us -> 3.3 us
    gather x7 -> x0, local copies, waits for them, and re-layouts: 15.2 us -> none  [the longest x2 4.75 us: shards(): jnp.take(zenith_flat, own_index)[None, :]]
    all_gather x1 -> x0, blocking collectives: 12.2 us -> none  [carried_in(): gathered = lax.all_gather(part, axis)]
    ppermute x10 -> x5, starting transfers between devices: 17.4 us -> 8.59 us  [the longest x1 4.84 us: shards(): lax.ppermute(amount, 'lev', [(i, i + step) for i in range(size - step)])]
    ppermute x10 -> x5, waiting for transfers between devices: 14.7 us -> 6.41 us  [the longest x4 5.04 us: swap(): return lax.ppermute(value, axis, route)]
    scatter-add x1 -> x0, other arithmetic: 7.62 us -> none  [shards(): jnp.nonzero(flat_lit, size=columns, fill_value=0)[0].astype(jnp.int32)]
    dot_general x10 -> x0, matrix products: 6 us -> none  [the longest x1 2.77 us: radiate(): jnp.einsum('kgc,g->kc', absorbed, solar_weight, precision=high) / layers]
    select_n x9 -> x0, other arithmetic: 3.46 us -> none  [the longest x1 1.05 us: shards(): jnp.take(zenith_flat, own_index)[None, :]]
    pallas_call x0 -> x3, Pallas kernels: none -> 3.3 us  [the longest x1 1.66 us: shards(): pl.pallas_call(radiate_kernel, out_shape=tile(levels), scratch_shapes=[pl...]
  transfers between devices with their start and end apart: 10 -> 5, of which waited for: 5 -> 4; matrix products, arithmetic and copies ran while one was open for 11% -> 0% of each run, Pallas kernels for 0% -> 8%
where the time goes in v1:
time: 21 us; the launch traced here: 20.8 us
  starting transfers between devices  8.59 us (41%)
  waiting for transfers between devices  6.41 us (31%)
  Pallas kernels  3.3 us (16%)
  other arithmetic  0.96 us (5%)
  between operations  0.77 us (4%)
  local copies, waits for them, and re-layouts  0.76 us (4%)
    ppermute x4, waiting for transfers between devices, swap(): return lax.ppermute(value, axis, route)  5.04 us
    ppermute x1, starting transfers between devices, shards(): lax.ppermute(amount, 'lev', [(i, i + step) for i in range(size - step)])  4.84 us
    ppermute x4, starting transfers between devices, swap(): return lax.ppermute(value, axis, route)  3.74 us
    pallas_call x1, Pallas kernels, shards(): pl.pallas_call(radiate_kernel, out_shape=tile(levels), scratch_shapes=[pl...  1.66 us
    pallas_call x1, Pallas kernels, shards(): pl.pallas_call(step_kernel, out_shape=tile(levels), compiler_params=big,...  1.53 us
    ppermute x1, waiting for transfers between devices, shards(): lax.ppermute(amount, 'lev', [(i, i + step) for i in range(size - step)])  1.37 us
    reduce_sum x1, other arithmetic, shards(): amount = jnp.sum(absorber, axis=1)  0.95 us
    unnamed x18, local copies, waits for them, and re-layouts  0.76 us
  transfers between devices with their start and end apart: 5, of which 4 were waited for; matrix products, arithmetic and copies ran while one was open for 0% of the time, Pallas kernels for 8%

profile of v1, /device:TPU:0, one launch (start us, length us, event | category | flops | bytes accessed | tf_op | source)
XLA Modules:
  0.0 20.8 jit_solution(15332441419004626902)
XLA Ops:
  0.6 0.0 copy-start
  0.6 0.0 copy-start.7
  0.6 0.0 copy-start.8
  0.7 1.0 %reduce_sum.9 = f32[7,8,128]{2,1,0:T(8,128)S(1)} reduce(f32[7,4,8,128]{3,2,1,0:T(8,128)} %absorber.1, f32[]{:T(128)} %constant.0.clone.1), dimensions={1}, to_apply=%region_0.0 | reduce | flops 21504 | bytes 143364 | tf_op jit(solution)/shard_map/reduce_sum | solution.py:261
  1.6 4.8 %collective-permute-start = (f32[7,8,128]{2,1,0:T(8,128)S(1)}, f32[7,8,128]{2,1,0:T(8,128)S(1)}, u32[]{:S(2)}, u32[]{:S(2)}) collective-permute-start(f32[7,8,128]{2,1,0:T(8,128)S(1)} %reduce_sum.9), channel_id=1, source_target_pairs={{0,2},{1,3},{4,6},{5,7},{8,10},{9,11},{12,14},{13,15},{16,18},{17,... | collective-permute-start | bytes 86024 | tf_op jit(solution)/shard_map/ppermute | solution.py:265
  6.5 0.0 copy-done.7
  6.5 0.0 copy-done.8
  6.5 0.0 copy-start.2
  6.5 0.0 copy-start.3
  6.5 0.0 copy-start.4
  6.5 0.0 copy-start.5
  6.5 0.0 copy-start.6
  6.6 0.1 collective-permute-start.1
  6.6 1.4 %collective-permute-done.upper = f32[7,8,128]{2,1,0:T(8,128)S(1)} collective-permute-done((f32[7,8,128]{2,1,0:T(8,128)S(1)}, f32[7,8,128]{2,1,0:T(8,128)S(1)}, u32[]{:S(2)}, u32[]{:S(2)}) %collective-permute-start) | collective-permute-done | bytes 28704 | tf_op jit(solution)/shard_map/ppermute | solution.py:265
  8.0 0.0 copy-done
  8.0 0.0 copy-done.2
  8.0 0.0 copy-done.3
  8.0 0.0 copy-done.4
  8.0 0.0 copy-done.5
  8.0 0.0 copy-done.6
  8.0 1.7 %radiate.1.own_heat = f32[4,8,128]{2,1,0:T(8,128)} custom-call(f32[7,4,8,128]{3,2,1,0:T(8,128)S(1)} %copy-done, f32[7,8,128]{2,1,0:T(8,128)S(1)} %collective-permute-done.upper, f32[8,128]{1,0:T(8,128)S(1)} %copy-done.4, s32[8,128]{1,0:T(8,128)S(1)} %copy-done.5, f32[4,8,128]{2,1,0:T(8,128)S(1)} %copy-done.2, f32[7,224]{1,0:T(8,128)S(1)} %copy-done.3, ...), custom_call_target="tpu_custom_call" | custom-call | tf_op jit(solution)/shard_map/radiate/pallas_call | solution.py:266
  9.7 0.0 collective-permute-start.2
  9.7 0.0 collective-permute-done.1.other_state
  9.7 1.4 %collective-permute-done.2.other_heat = f32[4,8,128]{2,1,0:T(8,128)S(1)} collective-permute-done((f32[4,8,128]{2,1,0:T(8,128)}, f32[4,8,128]{2,1,0:T(8,128)S(1)}, u32[]{:S(2)}, u32[]{:S(2)}) %collective-permute-start.2) | collective-permute-done | bytes 16416 | tf_op jit(solution)/shard_map/ppermute | solution.py:249
  11.1 0.0 copy-start.1
  11.1 0.7 %copy-done.1 = f32[4,8,128]{2,1,0:T(8,128)S(1)} copy-done((f32[4,8,128]{2,1,0:T(8,128)S(1)}, f32[4,8,128]{2,1,0:T(8,128)}, u32[]{:S(2)}) %copy-start.1) | copy-done | bytes 16408
  11.8 0.1 pack.1
  11.9 3.7 %collective-permute-start.3 = (f32[2,8,128]{2,1,0:T(8,128)S(1)}, f32[2,8,128]{2,1,0:T(8,128)S(1)}, u32[]{:S(2)}, u32[]{:S(2)}) collective-permute-start(f32[2,8,128]{2,1,0:T(8,128)S(1)} %get-tuple-element.4), channel_id=1, source_target_pairs={{4,8},{12,0},{8,4},{0,12},{5,9},{13,1},{9,5},{1,13},{6,10},{14,2},... | collective-permute-start | bytes 24584 | tf_op jit(solution)/shard_map/ppermute | solution.py:249
  15.6 0.0 collective-permute-start.4
  15.6 1.8 %collective-permute-done.3.got_one = f32[2,8,128]{2,1,0:T(8,128)S(1)} collective-permute-done((f32[2,8,128]{2,1,0:T(8,128)S(1)}, f32[2,8,128]{2,1,0:T(8,128)S(1)}, u32[]{:S(2)}, u32[]{:S(2)}) %collective-permute-start.3) | collective-permute-done | bytes 8224 | tf_op jit(solution)/shard_map/ppermute | solution.py:249
  17.4 1.8 %collective-permute-done.4.got_two = f32[2,8,128]{2,1,0:T(8,128)S(1)} collective-permute-done((f32[2,8,128]{2,1,0:T(8,128)S(1)}, f32[2,8,128]{2,1,0:T(8,128)S(1)}, u32[]{:S(2)}, u32[]{:S(2)}) %collective-permute-start.4) | collective-permute-done | bytes 8224 | tf_op jit(solution)/shard_map/ppermute | solution.py:249
  19.2 1.5 %step.1 = f32[4,8,128]{2,1,0:T(8,128)} custom-call(f32[5,8,128]{2,1,0:T(8,128)S(1)} %pad_maximum_fusion.own_state, f32[4,8,128]{2,1,0:T(8,128)S(1)} %copy-done.1, f32[5,8,128]{2,1,0:T(8,128)S(1)} %collective-permute-done.1.other_state, f32[4,8,128]{2,1,0:T(8,128)S(1)} %collective-permute-done.2.other_heat, f32[2,8,128]{2,1,0:T(8,128)S(1)} %collective-permute-done.3.got_one, ...), custom_call_target="tpu_custom_call" | custom-call | tf_op jit(solution)/shard_map/step/pallas_call | solution.py:284
  (1 shorter events, 0.0 us)
Async XLA Ops:
  0.6 7.4 %copy-start = (f32[7,4,8,128]{3,2,1,0:T(8,128)S(1)}, f32[7,4,8,128]{3,2,1,0:T(8,128)}, u32[]{:S(2)}) copy-start(f32[7,4,8,128]{3,2,1,0:T(8,128)} %absorber.1) | copy-start | bytes 344068
  0.6 5.8 %copy-start.7 = (f32[4,8,128]{2,1,0:T(8,128)S(1)}, f32[4,8,128]{2,1,0:T(8,128)}, u32[]{:S(2)}) copy-start(f32[4,8,128]{2,1,0:T(8,128)} %param.8) | copy-start | bytes 49156
  0.6 5.8 %copy-start.8 = (f32[8,128]{1,0:T(8,128)S(1)}, f32[8,128]{1,0:T(8,128)}, u32[]{:S(2)}) copy-start(f32[8,128]{1,0:T(8,128)} %param.9) | copy-start | bytes 12292
  1.6 6.4 %collective-permute-start = (f32[7,8,128]{2,1,0:T(8,128)S(1)}, f32[7,8,128]{2,1,0:T(8,128)S(1)}, u32[]{:S(2)}, u32[]{:S(2)}) collective-permute-start(f32[7,8,128]{2,1,0:T(8,128)S(1)} %reduce_sum.9), channel_id=1, source_target_pairs={{0,2},{1,3},{4,6},{5,7},{8,10},{9,11},{12,14},{13,15},{16,18},{17,... | collective-permute-start | bytes 86024 | tf_op jit(solution)/shard_map/ppermute | solution.py:265
  6.5 1.5 %copy-start.2 = (f32[4,8,128]{2,1,0:T(8,128)S(1)}, f32[4,8,128]{2,1,0:T(8,128)}, u32[]{:S(2)}) copy-start(f32[4,8,128]{2,1,0:T(8,128)} %thickness.1) | copy-start | bytes 49156
  6.5 1.5 %copy-start.3 = (f32[7,224]{1,0:T(8,128)S(1)}, f32[7,224]{1,0:T(8,128)}, u32[]{:S(2)}) copy-start(f32[7,224]{1,0:T(8,128)} %coef.1) | copy-start | bytes 18820
  6.5 1.5 %copy-start.4 = (f32[8,128]{1,0:T(8,128)S(1)}, f32[8,128]{1,0:T(8,128)}, u32[]{:S(2)}) copy-start(f32[8,128]{1,0:T(8,128)} %zenith.1) | copy-start | bytes 12292
  6.5 1.5 %copy-start.5 = (s32[8,128]{1,0:T(8,128)S(1)}, s32[8,128]{1,0:T(8,128)}, u32[]{:S(2)}) copy-start(s32[8,128]{1,0:T(8,128)} %lit.1) | copy-start | bytes 12292
  6.5 1.5 %copy-start.6 = (f32[224]{0:T(256)S(1)}, f32[224]{0:T(256)}, u32[]{:S(2)}) copy-start(f32[224]{0:T(256)} %param.15) | copy-start | bytes 2692
  6.6 3.1 %collective-permute-start.1 = (f32[5,8,128]{2,1,0:T(8,128)S(1)}, f32[5,8,128]{2,1,0:T(8,128)S(1)}, u32[]{:S(2)}, u32[]{:S(2)}) collective-permute-start(f32[5,8,128]{2,1,0:T(8,128)S(1)} %pad_maximum_fusion.own_state), channel_id=1, source_target_pairs={{0,1},{1,0},{2,3},{3,2},{4,5},{5,4},{6,7},{7,6},{8,9},{9,8},{10,11... | collective-permute-start | bytes 61448 | tf_op jit(solution)/shard_map/ppermute | solution.py:249
  9.7 1.4 %collective-permute-start.2 = (f32[4,8,128]{2,1,0:T(8,128)}, f32[4,8,128]{2,1,0:T(8,128)S(1)}, u32[]{:S(2)}, u32[]{:S(2)}) collective-permute-start(f32[4,8,128]{2,1,0:T(8,128)} %radiate.1.own_heat), channel_id=1, source_target_pairs={{0,1},{1,0},{2,3},{3,2},{4,5},{5,4},{6,7},{7,6},{8,9},{9,8},{10,11... | collective-permute-start | bytes 49160 | tf_op jit(solution)/shard_map/ppermute | solution.py:249
  11.1 0.7 %copy-start.1 = (f32[4,8,128]{2,1,0:T(8,128)S(1)}, f32[4,8,128]{2,1,0:T(8,128)}, u32[]{:S(2)}) copy-start(f32[4,8,128]{2,1,0:T(8,128)} %radiate.1.own_heat) | copy-start | bytes 49156
  11.9 5.5 %collective-permute-start.3 = (f32[2,8,128]{2,1,0:T(8,128)S(1)}, f32[2,8,128]{2,1,0:T(8,128)S(1)}, u32[]{:S(2)}, u32[]{:S(2)}) collective-permute-start(f32[2,8,128]{2,1,0:T(8,128)S(1)} %get-tuple-element.4), channel_id=1, source_target_pairs={{4,8},{12,0},{8,4},{0,12},{5,9},{13,1},{9,5},{1,13},{6,10},{14,2},... | collective-permute-start | bytes 24584 | tf_op jit(solution)/shard_map/ppermute | solution.py:249
  15.6 3.7 %collective-permute-start.4 = (f32[2,8,128]{2,1,0:T(8,128)S(1)}, f32[2,8,128]{2,1,0:T(8,128)S(1)}, u32[]{:S(2)}, u32[]{:S(2)}) collective-permute-start(f32[2,8,128]{2,1,0:T(8,128)S(1)} %get-tuple-element.5), channel_id=1, source_target_pairs={{0,4},{8,12},{4,0},{12,8},{1,5},{9,13},{5,1},{13,9},{2,6},{10,14},... | collective-permute-start | bytes 24584 | tf_op jit(solution)/shard_map/ppermute | solution.py:249
